TPU v7x, 32 devices: a whole 2x2x4 slice. The times are simulated.
32 devices in a mesh: group: 2 (over y), lender: 4 (over z), tensor: 4 (over x, core).
Axes of the slice: x: 2, y: 2, z: 4, core: 2. Of those that a mesh axis runs over, the one named last changes fastest.
Arguments:
- activations: bfloat16 [16, 8192], P('group', 'lender'), parts along dimension 0, may hold values from -400 to 400
- norm_gain: bfloat16 [8192], P('lender'), may hold values from 0.099609375 to 1.8984375
- w_query: bfloat16 [8192, 8192], P('lender', 'tensor'), may hold values from -0.0625 to 0.0625
- w_out: bfloat16 [8192, 8192], P('tensor', 'lender'), may hold values from -0.0625 to 0.0625
- key_pool: bfloat16 [8, 256, 128, 128], P('tensor', ('group', 'lender')), parts along dimension 1, may hold values from -800 to 800
- value_block_store: bfloat16 [8, 256, 128, 128], P('tensor', ('group', 'lender')), parts along dimension 1, may hold values from -48 to 48
- block_list: int32 [16, 8, 16], P('group', 'tensor'), parts along dimension 0, may hold values from 0 to 127, as said below
- block_slot_table: int32 [8, 256], P('tensor', 'group'), parts along dimension 1, may hold values from 0 to 127, each once within a row
- kept_len: int32 [16, 8], P('group', 'tensor'), parts along dimension 0, may hold values from 1 to 16, as said below
Outputs:
- output: bfloat16 [16, 8192], P(('group', 'tensor'), 'lender'), parts along dimension 0
There are 2 independent parts, one for each index of `group`. A program takes and returns all parts, laid end to end along the dimension named above; an argument that names none is the same for every part. Nothing has to cross between parts.
Inputs may be any that keep to these rules, and one draw needn't show every extreme that they name: `block_list`: for each KV head, no logical block appears twice among all rows' lists. `kept_len`: some row of every KV head keeps 16 blocks and some other row keeps one.
All inputs are finite; a program needn't handle non-finite values.
Results may differ from a plain program's by a relative error of at most 0.012.
The roundings to bfloat16 on the way count: a program that leaves them out, or rounds other values in their place, can miss the bound.
Values may be sent and summed in bfloat16 or wider, within the bound.
A program may use at most 64 MiB of HBM per device.

v0:
```python
import jax
import jax.numpy as jnp
from jax import lax
from jax.sharding import PartitionSpec as P

D = 8192


very_low = -1e30
epsilon = 1e-05


def per_device(
    activations,
    norm_gain,
    w_query,
    w_out,
    key_pool,
    value_block_store,
    block_list,
    block_slot_table,
    kept_len,
):
    row_count = activations.shape[0]
    kv_heads = key_pool.shape[0]
    slot_count = key_pool.shape[1]
    head_dim = key_pool.shape[3]
    kept_most = block_list.shape[2]
    features = activations.astype(jnp.float32)
    squares = jnp.sum(features * features, axis=1)
    scaled = (features * norm_gain.astype(jnp.float32)).astype(jnp.bfloat16)
    partial_value = jnp.dot(scaled, w_query, preferred_element_type=jnp.float32)
    projected, square_sum = lax.psum((partial_value, squares), "lender")
    inverse = lax.rsqrt(square_sum / D + epsilon)
    query_vectors = (projected * inverse[:, None] * head_dim ** (-0.5)).astype(jnp.bfloat16)
    group_size = query_vectors.shape[1] // (kv_heads * head_dim)
    query_vectors = query_vectors.reshape(row_count, kv_heads, group_size, head_dim)
    slot_lookup_table = jnp.broadcast_to(
        block_slot_table[None], (row_count,) + block_slot_table.shape
    )
    slot_ids = jnp.take_along_axis(slot_lookup_table, block_list, axis=2)
    positions = jnp.arange(kept_most, dtype=jnp.int32)
    is_live = positions[None, None, :] < kept_len[:, :, None]
    local_slot = slot_ids - lax.axis_index("lender") * slot_count
    matches = is_live[..., None] & (
        local_slot[..., None] == jnp.arange(slot_count, dtype=jnp.int32)
    )
    owner_mask = jnp.transpose(jnp.any(matches, axis=2), (1, 2, 0))
    owner_half = owner_mask.astype(jnp.bfloat16)
    owner_full = owner_mask.astype(jnp.float32)
    used_slot = jnp.any(owner_mask, axis=2)
    picked = jnp.einsum(
        "hsr,rhgd->hsgd", owner_half, query_vectors, preferred_element_type=jnp.float32
    ).astype(jnp.bfloat16)
    scores = jnp.einsum("hsgd,hstd->hsgt", picked, key_pool, preferred_element_type=jnp.float32)
    block_best = jnp.max(scores, axis=3)
    spread = jnp.where(owner_mask[..., None], block_best[:, :, None, :], very_low)
    row_best = jnp.max(spread, axis=1)
    slot_best = jnp.max(jnp.where(owner_mask[..., None], row_best[:, None, :, :], very_low), axis=2)
    slot_best = jnp.where(used_slot[..., None], slot_best, 0.0)
    weights_full = jnp.where(
        used_slot[:, :, None, None], jnp.exp(scores - slot_best[..., None]), 0.0
    )
    slot_weight = jnp.sum(weights_full, axis=3)
    slot_value = jnp.einsum(
        "hsgt,hstd->hsgd",
        weights_full.astype(jnp.bfloat16),
        value_block_store,
        preferred_element_type=jnp.float32,
    )
    row_weight = jnp.einsum(
        "hsr,hsg->rhg", owner_full, slot_weight, precision=lax.Precision.HIGHEST
    )
    row_value = jnp.einsum(
        "hsr,hsgd->rhgd", owner_full, slot_value, precision=lax.Precision.HIGHEST
    )
    row_high = jnp.transpose(row_best, (1, 0, 2))
    lenders = lax.axis_size("lender")
    home_rows = row_count // lenders
    came_best, came_weight, came_value = (
        lax.all_to_all(row_high, "lender", split_axis=0, concat_axis=0, tiled=True),
        lax.all_to_all(row_weight, "lender", split_axis=0, concat_axis=0, tiled=True),
        lax.all_to_all(row_value, "lender", split_axis=0, concat_axis=0, tiled=True),
    )
    came_best = came_best.reshape((lenders, home_rows) + came_best.shape[1:])
    came_weight = came_weight.reshape((lenders, home_rows) + came_weight.shape[1:])
    came_value = came_value.reshape((lenders, home_rows) + came_value.shape[1:])
    highest = jnp.max(came_best, axis=0)
    factor = jnp.exp(came_best - highest[None])
    home_weight = jnp.sum(came_weight * factor, axis=0)
    home_value = jnp.sum(came_value * factor[..., None], axis=0)
    home_attended = (
        (home_value / home_weight[..., None]).astype(jnp.bfloat16).reshape(home_rows, -1)
    )
    attended = lax.all_gather(home_attended, "lender", axis=0, tiled=True)
    result = lax.psum_scatter(
        jnp.dot(attended, w_out, preferred_element_type=jnp.float32),
        "tensor",
        scatter_dimension=0,
        tiled=True,
    )
    return result.astype(jnp.bfloat16)


def solution(mesh):
    in_specs = (
        P("group", "lender"),
        P("lender"),
        P("lender", "tensor"),
        P("tensor", "lender"),
        P("tensor", ("group", "lender"), None, None),
        P("tensor", ("group", "lender"), None, None),
        P("group", "tensor", None),
        P("tensor", "group"),
        P("group", "tensor"),
    )
    out_specs = P(("group", "tensor"), "lender")
    return jax.shard_map(
        per_device, mesh=mesh, in_specs=in_specs, out_specs=out_specs, check_vma=False
    )
```

profile of v0, /device:TPU:0, one launch (start us, length us, event | category | flops | bytes accessed | tf_op | source)
XLA Modules:
  0.0 115.9 jit_solution(14642296983015357791)
XLA Ops:
  6.5 0.0 copy-start
  6.5 0.0 all-reduce.3.cloned.1.call-start
  6.6 0.8 convert_element_type.31
  7.4 5.2 %fusion.15 = f32[8,2048]{1,0:T(8,128)} fusion(bf16[2048,2048]{1,0:T(8,128)(2,1)} %param.11, bf16[8,2048]{1,0:T(8,128)(2,1)} %param.9, f32[2048]{0:T(1024)S(1)} %convert_element_type.31), kind=kOutput, calls=%fused_computation.26 | convolution fusion | flops 67158016 | bytes 8495104 | tf_op jit(solution)/shard_map/dot_general | solution.py:32
  12.7 0.0 all-reduce.3.cloned.1.call-update
  12.7 0.0 copy-done.1
  12.7 0.1 fusion.13
  12.8 0.0 copy-done.2
  12.9 0.1 reshape.57
  12.9 0.0 copy-done.3
  13.0 2.6 %gather_fusion = s32[256]{0:T(256)S(1)} fusion(s32[8,2,128]{2,1,0:T(2,128)S(1)} %broadcast_in_dim.66, s32[256]{0:T(256)S(1)} %reshape.57), kind=kCustom, calls=%fused_computation | custom fusion | bytes 5120 | tf_op jit(solution)/shard_map/jit(take_along_axis)/gather | solution.py:41
  15.6 0.1 reshape.60
  15.6 0.0 copy-done.4
  15.7 0.1 copy.48
  15.7 0.1 iota_compare_fusion.1
  15.8 13.5 %psum.15 = f32[8]{0:T(128)S(1)} all-reduce(f32[8]{0:T(128)S(1)} %fusion.13), channel_id=1, replica_groups=mesh['group'=2,'lender'=4,'tensor'=4] {'lender'}, use_global_device_ids=true, to_apply=%region_4.5 | all-reduce | flops 8 | bytes 64 | tf_op jit(solution)/shard_map/psum | solution.py:33
  29.3 0.2 fusion.10
  29.5 0.0 copy-done.5
  29.5 0.6 dynamic-slice
  30.8 18.7 %all-reduce.3.cloned.1.call-done = f32[8,2048]{1,0:T(8,128)} async-done(((f32[8,2048]{1,0:T(8,128)}), f32[8,2048]{1,0:T(8,128)}) %all-reduce.3.cloned.1.call-update) | async-done | bytes 65552 | tf_op jit(solution)/shard_map/psum | solution.py:33
  49.5 0.9 multiply_convert_fusion
  50.4 0.2 convolution_convert_fusion
  50.7 1.3 %fusion.22 = (f32[2,32,8]{2,1,0:T(8,128)S(1)}, f32[2,32,8,128]{3,2,1,0:T(8,128)S(1)}) fusion(bf16[2,32,128,128]{3,2,1,0:T(8,128)(2,1)S(1)} %copy-done, bf16[2,32,8,128]{3,1,2,0:T(8,128)(2,1)S(1)} %convolution_convert_fusion), kind=kOutput, calls=%fused_computation.43 | convolution fusion | flops 16842240 | bytes 2492416 | tf_op jit(solution)/shard_map/hsgd,hstd->hsgt/dot_general | solution.py:55
  52.0 0.1 copy.52
  52.0 0.1 select_reduce_fusion.1
  52.1 0.1 select_reduce_fusion
  52.2 0.1 copy.53
  52.3 0.6 copy.57
  52.9 3.4 %all-to-all-start.1 = ((f32[8,2,8]{2,1,0:T(2,128)}), f32[8,2,8]{2,1,0:T(2,128)S(1)}, u32[]{:S(2)}, u32[]{:S(2)}) async-start(f32[8,2,8]{2,1,0:T(2,128)} %copy.57), calls=%async_computation.1 | async-start | bytes 16384 | tf_op jit(solution)/shard_map/all_to_all | solution.py:81
  56.3 0.3 fusion.1
  56.6 2.3 %fusion.3 = f32[2,32,8,128]{3,2,1,0:T(8,128)S(1)} fusion(bf16[2,32,128,128]{3,2,1,0:T(8,128)(2,1)} %param.14, f32[2,32,8,128]{3,2,1,0:T(8,128)S(1)} %get-tuple-element.8, f32[2,32,8]{2,1,0:T(8,128)S(1)} %copy.53, pred[2,32]{1,0:T(4,128)(4,1)S(1)} %bitcast_reduce_fusion), kind=kOutput, calls=%fused_computation.8 | convolution fusion | flops 16973824 | bytes 2623552 | tf_op jit(solution)/shard_map/hsgt,hstd->hsgd/dot_general | solution.py:65
  58.9 0.2 convolution_bitcast_fusion.1
  59.1 0.7 copy.63
  59.8 2.1 %all-to-all-done.1 = f32[8,2,8]{2,1,0:T(2,128)S(1)} async-done(((f32[8,2,8]{2,1,0:T(2,128)}), f32[8,2,8]{2,1,0:T(2,128)S(1)}, u32[]{:S(2)}, u32[]{:S(2)}) %all-to-all-start.1) | async-done | bytes 544 | tf_op jit(solution)/shard_map/all_to_all | solution.py:81
  61.9 3.2 %all-to-all-start.2 = ((f32[8,2,8]{2,1,0:T(2,128)}), f32[8,2,8]{2,1,0:T(2,128)S(1)}, u32[]{:S(2)}, u32[]{:S(2)}) async-start(f32[8,2,8]{2,1,0:T(2,128)} %copy.63), calls=%async_computation.2 | async-start | bytes 16384 | tf_op jit(solution)/shard_map/all_to_all | solution.py:82
  65.2 0.2 convolution_bitcast_fusion
  65.4 0.6 copy.56
  66.0 4.7 %all-to-all-done.2 = f32[8,2,8]{2,1,0:T(2,128)S(1)} async-done(((f32[8,2,8]{2,1,0:T(2,128)}), f32[8,2,8]{2,1,0:T(2,128)S(1)}, u32[]{:S(2)}, u32[]{:S(2)}) %all-to-all-start.2) | async-done | bytes 544 | tf_op jit(solution)/shard_map/all_to_all | solution.py:82
  70.7 3.3 %all-to-all-start = ((f32[8,2,8,128]{3,2,1,0:T(8,128)}), f32[8,2,8,128]{3,2,1,0:T(8,128)S(1)}, u32[]{:S(2)}, u32[]{:S(2)}) async-start(f32[8,2,8,128]{3,2,1,0:T(8,128)} %copy.56), calls=%async_computation | async-start | bytes 131072 | tf_op jit(solution)/shard_map/all_to_all | solution.py:83
  74.1 0.1 copy.59
  74.2 0.1 copy.65
  74.3 5.5 %all-to-all-done = f32[8,2,8,128]{3,2,1,0:T(8,128)S(1)} async-done(((f32[8,2,8,128]{3,2,1,0:T(8,128)}), f32[8,2,8,128]{3,2,1,0:T(8,128)S(1)}, u32[]{:S(2)}, u32[]{:S(2)}) %all-to-all-start) | async-done | bytes 65568 | tf_op jit(solution)/shard_map/all_to_all | solution.py:83
  79.8 0.1 fusion.14
  79.9 0.1 divide_convert_fusion
  80.0 13.1 %all-gather = bf16[4,2,2048]{2,1,0:T(2,128)(2,1)S(1)} all-gather(bf16[1,2,2048]{2,1,0:T(2,128)(2,1)S(1)} %bitcast.37), channel_id=1, replica_groups=mesh['group'=2,'lender'=4,'tensor'=4] {'lender'}, dimensions={0}, use_global_device_ids=true | all-gather | bytes 40960 | tf_op jit(solution)/shard_map/all_gather | solution.py:95
  93.2 4.6 %fusion.23 = f32[8,2048]{1,0:T(8,128)S(1)} fusion(bf16[8,2048]{1,0:T(8,128)(2,1)S(1)} %reshape.69, bf16[2048,2048]{1,0:T(8,128)(2,1)} %param.12), kind=kOutput, calls=%fused_computation.44 | convolution fusion | flops 67108864 | bytes 8486912 | tf_op jit(solution)/shard_map/dot_general | solution.py:97
  97.7 10.7 %all-reduce = bf16[8,2048]{1,0:T(8,128)(2,1)S(1)} all-reduce(f32[8,2048]{1,0:T(8,128)S(1)} %fusion.23), channel_id=2, replica_groups=mesh['group'=2,'lender'=4,'tensor'=4] {'tensor'}, use_global_device_ids=true, to_apply=%region_12.13.clone | all-reduce | flops 16384 | bytes 98304
  108.4 0.6 dynamic-slice_convert_fusion
  (18 shorter events, 0.2 us)
Async XLA Ops:
  6.5 44.1 %copy-start = (bf16[2,32,128,128]{3,2,1,0:T(8,128)(2,1)S(1)}, bf16[2,32,128,128]{3,2,1,0:T(8,128)(2,1)}, u32[]{:S(2)}) copy-start(bf16[2,32,128,128]{3,2,1,0:T(8,128)(2,1)} %param.13) | copy-start | bytes 6291460
  6.5 6.2 %copy-start.1 = (bf16[8,2048]{1,0:T(8,128)(2,1)S(1)}, bf16[8,2048]{1,0:T(8,128)(2,1)}, u32[]{:S(2)}) copy-start(bf16[8,2048]{1,0:T(8,128)(2,1)} %param.9) | copy-start | bytes 98308
  6.5 6.3 %copy-start.2 = (s32[8,2,16]{2,1,0:T(2,128)S(1)}, s32[8,2,16]{2,1,0:T(2,128)}, u32[]{:S(2)}) copy-start(s32[8,2,16]{2,1,0:T(2,128)} %param.15) | copy-start | bytes 3076
  6.5 6.4 %copy-start.3 = (s32[2,128]{1,0:T(2,128)S(1)}, s32[2,128]{1,0:T(2,128)}, u32[]{:S(2)}) copy-start(s32[2,128]{1,0:T(2,128)} %param.16) | copy-start | bytes 3076
  6.5 43.0 %all-reduce.3.cloned.1.call-start = ((), (), s32[]{:S(2)}) async-start(), calls=%async_computation.3 | async-start | bytes 131072 | tf_op jit(solution)/shard_map/psum | solution.py:33
  7.4 8.2 %copy-start.4 = (s32[8,2]{0,1:T(2,128)S(1)}, s32[8,2]{0,1:T(2,128)}, u32[]{:S(2)}) copy-start(s32[8,2]{0,1:T(2,128)} %param.17) | copy-start | bytes 196
  7.4 22.1 %copy-start.5 = (u32[32]{0:T(128)S(1)}, u32[32]{0:T(128)}, u32[]{:S(2)}) copy-start(u32[32]{0:T(128)} %constant.64) | copy-start | bytes 388
  52.9 9.0 %all-to-all-start.1 = ((f32[8,2,8]{2,1,0:T(2,128)}), f32[8,2,8]{2,1,0:T(2,128)S(1)}, u32[]{:S(2)}, u32[]{:S(2)}) async-start(f32[8,2,8]{2,1,0:T(2,128)} %copy.57), calls=%async_computation.1 | async-start | bytes 16384 | tf_op jit(solution)/shard_map/all_to_all | solution.py:81
  61.9 8.8 %all-to-all-start.2 = ((f32[8,2,8]{2,1,0:T(2,128)}), f32[8,2,8]{2,1,0:T(2,128)S(1)}, u32[]{:S(2)}, u32[]{:S(2)}) async-start(f32[8,2,8]{2,1,0:T(2,128)} %copy.63), calls=%async_computation.2 | async-start | bytes 16384 | tf_op jit(solution)/shard_map/all_to_all | solution.py:82
  70.7 9.1 %all-to-all-start = ((f32[8,2,8,128]{3,2,1,0:T(8,128)}), f32[8,2,8,128]{3,2,1,0:T(8,128)S(1)}, u32[]{:S(2)}, u32[]{:S(2)}) async-start(f32[8,2,8,128]{3,2,1,0:T(8,128)} %copy.56), calls=%async_computation | async-start | bytes 131072 | tf_op jit(solution)/shard_map/all_to_all | solution.py:83
Sparse Core Ops, SparseCore 0:
  12.8 36.6 all-reduce.2
where the time goes:
time: 116 us
  blocking collectives  37.3 us (32%)
  waiting for transfers between devices  31 us (27%)
  between operations  14.2 us (12%)
  matrix products  14 us (12%)
  starting transfers between devices  9.95 us (9%)
  local copies, waits for them, and re-layouts  6.38 us (6%)
  other arithmetic  2.96 us (3%)
    psum x1, waiting for transfers between devices, per_device(): projected, square_sum = lax.psum((partial_value, squares), 'lender')  18.7 us
    psum x1, blocking collectives, per_device(): projected, square_sum = lax.psum((partial_value, squares), 'lender')  13.5 us
    all_gather x1, blocking collectives, per_device(): attended = lax.all_gather(home_attended, 'lender', axis=0, tiled=True)  13.1 us
    unnamed x1, blocking collectives  10.7 us
    all_to_all x1, waiting for transfers between devices, per_device(): lax.all_to_all(row_value, 'lender', split_axis=0, concat_axis=0, tiled=True)  5.51 us
    dot_general x1, matrix products, per_device(): partial_value = jnp.dot(scaled, w_query, preferred_element_type=jnp.float32)  5.24 us
    all_to_all x1, waiting for transfers between devices, per_device(): lax.all_to_all(row_weight, 'lender', split_axis=0, concat_axis=0, tiled=T...  4.68 us
    dot_general x1, matrix products, per_device(): jnp.dot(attended, w_out, preferred_element_type=jnp.float32)  4.57 us
  transfers between devices with their start and end apart: 4, of which 4 were waited for; matrix products, arithmetic and copies ran while one was open for 7% of the time, Pallas kernels for 0%

commit v1 on v0

--- a/solution.py
+++ b/solution.py
@@ -1,16 +1,17 @@
+import functools
+
 import jax
 import jax.numpy as jnp
 from jax import lax
+from jax.experimental import pallas as pl
+from jax.experimental.pallas import tpu as pltpu
 from jax.sharding import PartitionSpec as P
-
-D = 8192
-
 
 very_low = -1e30
 epsilon = 1e-05
 
 
-def per_device(
+def separate_ops(
     activations,
     norm_gain,
     w_query,
@@ -31,7 +32,8 @@
     scaled = (features * norm_gain.astype(jnp.float32)).astype(jnp.bfloat16)
     partial_value = jnp.dot(scaled, w_query, preferred_element_type=jnp.float32)
     projected, square_sum = lax.psum((partial_value, squares), "lender")
-    inverse = lax.rsqrt(square_sum / D + epsilon)
+    width = features.shape[1] * lax.axis_size("lender")
+    inverse = lax.rsqrt(square_sum / width + epsilon)
     query_vectors = (projected * inverse[:, None] * head_dim ** (-0.5)).astype(jnp.bfloat16)
     group_size = query_vectors.shape[1] // (kv_heads * head_dim)
     query_vectors = query_vectors.reshape(row_count, kv_heads, group_size, head_dim)
@@ -102,6 +104,388 @@
     return result.astype(jnp.bfloat16)
 
 
+MESH = pl.DeviceIdType.MESH
+LANES = 128
+SUBLANES = 8
+
+
+def fused_kernel(
+    lenders,
+    tensors,
+    act_ref,
+    gain_ref,
+    list_ref,
+    table_ref,
+    kept_ref,
+    wq_hbm,
+    wo_hbm,
+    key_hbm,
+    value_hbm,
+    out_ref,
+    wq,
+    wo,
+    keys,
+    values,
+    q_send,
+    q_recv,
+    q_all,
+    bias,
+    scores,
+    part_send,
+    part_recv,
+    att_all,
+    sum_send,
+    sum_recv,
+    wq_sem,
+    wo_sem,
+    kv_sem,
+    lender_send,
+    lender_recv,
+    tensor_send,
+    tensor_recv,
+):
+    me = lax.axis_index("lender")
+    mine = lax.axis_index("tensor")
+    rows = act_ref.shape[0]
+    kv_heads, slot_count, tokens, head_dim = keys.shape
+    width = wq.shape[2]
+    chunk_heads = width // head_dim
+    chunk_rows = chunk_heads * rows
+    group = wo.shape[0] * chunk_heads // kv_heads
+    chunks_per_kv = group // chunk_heads
+    kept_most = list_ref.shape[1] // kv_heads
+    f32, bf16 = jnp.float32, jnp.bfloat16
+
+    def lender_at(offset):
+        return lax.rem(me + offset, lenders)
+
+    wq_copies = []
+    for offset in list(range(1, lenders)) + [0]:
+        columns = pl.ds(pl.multiple_of(lender_at(offset) * width, width), width)
+        wq_copies.append(
+            pltpu.make_async_copy(wq_hbm.at[:, columns], wq.at[offset], wq_sem.at[offset])
+        )
+    key_copy = pltpu.make_async_copy(key_hbm, keys, kv_sem.at[0])
+    value_copy = pltpu.make_async_copy(value_hbm, values, kv_sem.at[1])
+    wo_copies = []
+    for offset in range(lenders):
+        source = lender_at(lenders - offset)
+        lines = pl.ds(pl.multiple_of(source * width, width), width)
+        wo_copies.append(
+            pltpu.make_async_copy(wo_hbm.at[lines], wo.at[offset], wo_sem.at[offset])
+        )
+    for copy in wq_copies:
+        copy.start()
+
+    barrier = pltpu.get_barrier_semaphore()
+    for offset in range(1, lenders):
+        pl.semaphore_signal(
+            barrier, inc=1, device_id={"lender": lender_at(offset)}, device_id_type=MESH
+        )
+    for offset in range(1, tensors):
+        pl.semaphore_signal(
+            barrier,
+            inc=1,
+            device_id={"tensor": lax.rem(mine + offset, tensors)},
+            device_id_type=MESH,
+        )
+
+    def to_lender(stage, offset, src, dst):
+        return pltpu.make_async_remote_copy(
+            src_ref=src,
+            dst_ref=dst,
+            send_sem=lender_send.at[stage, offset],
+            recv_sem=lender_recv.at[stage, offset],
+            device_id={"lender": lender_at(offset)},
+            device_id_type=MESH,
+        )
+
+    features = act_ref[...].astype(f32)
+    squares = jnp.sum(features * features, axis=1, keepdims=True)
+    scaled = (features * gain_ref[...].astype(f32)).astype(bf16)
+
+    blocks = table_ref.shape[1]
+    block_ids = lax.broadcasted_iota(jnp.int32, (rows, blocks), 1)
+    local_slots = lax.broadcasted_iota(jnp.int32, (slot_count, blocks), 0) + me * slot_count
+    for h in range(kv_heads):
+        member = jnp.zeros((rows, blocks), f32)
+        for k in range(kept_most):
+            at = h * kept_most + k
+            hit = (list_ref[:, at : at + 1] == block_ids) & (kept_ref[:, h : h + 1] > k)
+            member = jnp.where(hit, 1.0, member)
+        holds = jnp.where(table_ref[h : h + 1, :] == local_slots, 1.0, 0.0)
+        owner = lax.dot_general(
+            member.astype(bf16),
+            holds.astype(bf16),
+            (((1,), (1,)), ((), ())),
+            preferred_element_type=f32,
+        )
+        lowered = (owner - 1.0) * -very_low
+        for s in range(slot_count):
+            bias[h, :, s * tokens : (s + 1) * tokens] = jnp.broadcast_to(
+                lowered[:, s : s + 1], (rows, tokens)
+            )
+
+    started = []
+    own_partial = None
+    for at, offset in enumerate(list(range(1, lenders)) + [0]):
+        wq_copies[at].wait()
+        if at == 0:
+            key_copy.start()
+            value_copy.start()
+        if at == min(1, lenders - 1):
+            for copy in wo_copies:
+                copy.start()
+        partial = jnp.dot(scaled, wq[offset], preferred_element_type=f32)
+        if offset == 0:
+            own_partial = partial
+            continue
+        q_send[offset, :, :width] = partial
+        q_send[offset, :, width:] = jnp.broadcast_to(squares, (rows, LANES))
+        if at == 0:
+            pl.semaphore_wait(barrier, lenders + tensors - 2)
+        copy = to_lender(0, offset, q_send.at[offset], q_recv.at[offset])
+        copy.start()
+        started.append(copy)
+
+    projected, square_sum = own_partial, squares
+    for copy in started:
+        copy.wait_recv()
+    for offset in range(1, lenders):
+        projected = projected + q_recv[offset, :, :width]
+        square_sum = square_sum + q_recv[offset, :, width : width + 1]
+    inverse = lax.rsqrt(square_sum / (act_ref.shape[1] * lenders) + epsilon)
+    normed = projected * inverse * head_dim ** (-0.5)
+    q_all[me] = jnp.concatenate(
+        [normed[:, j * head_dim : (j + 1) * head_dim] for j in range(chunk_heads)], axis=0
+    ).astype(bf16)
+    q_copies = []
+    for offset in range(1, lenders):
+        copy = to_lender(1, offset, q_all.at[me], q_all.at[me])
+        copy.start()
+        q_copies.append(copy)
+    key_copy.wait()
+    for copy in q_copies:
+        copy.wait_recv()
+    started += q_copies
+
+    step_slots = max(1, min(slot_count, 512 // tokens))
+    step = step_slots * tokens
+    steps = slot_count // step_slots
+    high = []
+    for h in range(kv_heads):
+        queries = q_all[h * chunks_per_kv : (h + 1) * chunks_per_kv].reshape(
+            group * rows, head_dim
+        )
+        running = None
+        for c in range(steps):
+            block = keys[h, c * step_slots : (c + 1) * step_slots].reshape(step, head_dim)
+            found = lax.dot_general(
+                queries, block, (((1,), (1,)), ((), ())), preferred_element_type=f32
+            )
+            found = found.reshape(group, rows, step) + bias[h, :, c * step : (c + 1) * step][None]
+            found = found.reshape(group * rows, step)
+            scores[h, :, c * step : (c + 1) * step] = found
+            for t in range(0, step, LANES):
+                piece = found[:, t : t + LANES]
+                running = piece if running is None else jnp.maximum(running, piece)
+        high.append(jnp.max(running, axis=1, keepdims=True))
+    value_copy.wait()
+
+    eye = lax.broadcasted_iota(jnp.int32, (chunk_rows, LANES), 0) == lax.broadcasted_iota(
+        jnp.int32, (chunk_rows, LANES), 1
+    )
+    first_line = lax.broadcasted_iota(jnp.int32, (SUBLANES, LANES), 0) == 0
+    for h in range(kv_heads):
+        best = high[h]
+        total = None
+        gathered = jnp.zeros((group * rows, head_dim), f32)
+        for c in range(steps):
+            weights = jnp.exp(scores[h, :, c * step : (c + 1) * step] - best)
+            for t in range(0, step, LANES):
+                piece = weights[:, t : t + LANES]
+                total = piece if total is None else total + piece
+            block = values[h, c * step_slots : (c + 1) * step_slots].reshape(step, head_dim)
+            gathered = gathered + jnp.dot(
+                weights.astype(bf16), block, preferred_element_type=f32
+            )
+        total = jnp.sum(total, axis=1, keepdims=True)
+        for j in range(chunks_per_kv):
+            lines = slice(j * chunk_rows, (j + 1) * chunk_rows)
+            d = h * chunks_per_kv + j
+            best_line = jnp.sum(jnp.where(eye, best[lines], 0.0), axis=0, keepdims=True)
+            total_line = jnp.sum(jnp.where(eye, total[lines], 0.0), axis=0, keepdims=True)
+            part_send[d, :chunk_rows, :] = gathered[lines]
+            part_send[d, chunk_rows:, :] = jnp.where(first_line, best_line, total_line)
+
+    part_copies = []
+    for offset in range(1, lenders):
+        copy = to_lender(2, offset, part_send.at[lender_at(offset)], part_recv.at[offset])
+        copy.start()
+        part_copies.append(copy)
+    started += part_copies
+    part_recv[0] = part_send[me]
+    for copy in part_copies:
+        copy.wait_recv()
+    bests, totals = [], []
+    for offset in range(lenders):
+        line = part_recv[offset, chunk_rows : chunk_rows + 1, :]
+        bests.append(jnp.sum(jnp.where(eye, line, 0.0), axis=1, keepdims=True))
+        line = part_recv[offset, chunk_rows + 1 : chunk_rows + 2, :]
+        totals.append(jnp.sum(jnp.where(eye, line, 0.0), axis=1, keepdims=True))
+    highest = functools.reduce(jnp.maximum, bests)
+    home_total = jnp.zeros((chunk_rows, 1), f32)
+    home_value = jnp.zeros((chunk_rows, head_dim), f32)
+    for offset in range(lenders):
+        factor = jnp.exp(bests[offset] - highest)
+        home_total = home_total + totals[offset] * factor
+        home_value = home_value + part_recv[offset, :chunk_rows, :] * factor
+    att_all[me] = (home_value / home_total).astype(bf16)
+    att_copies = []
+    for offset in range(1, lenders):
+        copy = to_lender(3, offset, att_all.at[me], att_all.at[me])
+        copy.start()
+        att_copies.append(copy)
+    started += att_copies
+
+    product = None
+    for offset in range(lenders):
+        wo_copies[offset].wait()
+        if offset > 0:
+            att_copies[offset - 1].wait_recv()
+        chunk = att_all[lender_at(lenders - offset)].astype(f32)
+        chunk = jnp.concatenate(
+            [chunk[j * rows : (j + 1) * rows] for j in range(chunk_heads)], axis=1
+        ).astype(bf16)
+        term = jnp.dot(chunk, wo[offset], preferred_element_type=f32)
+        product = term if product is None else product + term
+
+    home_rows = rows // tensors
+    part_width = product.shape[1] // tensors
+    line_block = lax.broadcasted_iota(jnp.int32, (rows, part_width), 0) // home_rows
+    for d in range(tensors):
+        packed = jnp.zeros((rows, part_width), f32)
+        for c in range(tensors):
+            piece = product[:, c * part_width : (c + 1) * part_width]
+            shift = (c - d) * home_rows % rows
+            if shift:
+                piece = pltpu.roll(piece, shift, 0)
+            packed = jnp.where(line_block == c, piece, packed)
+        sum_send[d] = packed
+    for offset in range(1, tensors):
+        target = lax.rem(mine + offset, tensors)
+        copy = pltpu.make_async_remote_copy(
+            src_ref=sum_send.at[target],
+            dst_ref=sum_recv.at[offset],
+            send_sem=tensor_send.at[offset],
+            recv_sem=tensor_recv.at[offset],
+            device_id={"tensor": target},
+            device_id_type=MESH,
+        )
+        copy.start()
+        started.append(copy)
+    result = sum_send[mine]
+    for copy in started[1 - tensors :] if tensors > 1 else []:
+        copy.wait_recv()
+    for offset in range(1, tensors):
+        result = result + sum_recv[offset]
+    for c in range(tensors):
+        out_ref[:, c * part_width : (c + 1) * part_width] = result[
+            c * home_rows : (c + 1) * home_rows
+        ].astype(out_ref.dtype)
+    for copy in started:
+        copy.wait_send()
+
+
+def fused(
+    activations,
+    norm_gain,
+    w_query,
+    w_out,
+    key_pool,
+    value_block_store,
+    block_list,
+    block_slot_table,
+    kept_len,
+):
+    lenders, tensors = lax.axis_size("lender"), lax.axis_size("tensor")
+    rows, depth = activations.shape
+    kv_heads, slot_count, tokens, head_dim = key_pool.shape
+    width = w_query.shape[1] // lenders
+    out_width = w_out.shape[1]
+    chunk_rows = width // head_dim * rows
+    group_rows = w_query.shape[1] // head_dim // kv_heads * rows
+    part_width = out_width // tensors
+    f32, bf16 = jnp.float32, jnp.bfloat16
+    vmem = pl.BlockSpec(memory_space=pltpu.VMEM)
+    hbm = pl.BlockSpec(memory_space=pl.ANY)
+    return pl.pallas_call(
+        functools.partial(fused_kernel, lenders, tensors),
+        out_shape=jax.ShapeDtypeStruct((rows // tensors, out_width), bf16),
+        in_specs=[vmem] * 5 + [hbm] * 4,
+        out_specs=vmem,
+        scratch_shapes=[
+            pltpu.VMEM((lenders, depth, width), bf16),
+            pltpu.VMEM((lenders, width, out_width), bf16),
+            pltpu.VMEM(key_pool.shape, bf16),
+            pltpu.VMEM(key_pool.shape, bf16),
+            pltpu.VMEM((lenders, rows, width + LANES), f32),
+            pltpu.VMEM((lenders, rows, width + LANES), f32),
+            pltpu.VMEM((lenders, chunk_rows, head_dim), bf16),
+            pltpu.VMEM((kv_heads, rows, slot_count * tokens), f32),
+            pltpu.VMEM((kv_heads, group_rows, slot_count * tokens), f32),
+            pltpu.VMEM((lenders, chunk_rows + SUBLANES, head_dim), f32),
+            pltpu.VMEM((lenders, chunk_rows + SUBLANES, head_dim), f32),
+            pltpu.VMEM((lenders, chunk_rows, head_dim), bf16),
+            pltpu.VMEM((tensors, rows, part_width), f32),
+            pltpu.VMEM((tensors, rows, part_width), f32),
+            pltpu.SemaphoreType.DMA((lenders,)),
+            pltpu.SemaphoreType.DMA((lenders,)),
+            pltpu.SemaphoreType.DMA((2,)),
+            pltpu.SemaphoreType.DMA((4, lenders)),
+            pltpu.SemaphoreType.DMA((4, lenders)),
+            pltpu.SemaphoreType.DMA((tensors,)),
+            pltpu.SemaphoreType.DMA((tensors,)),
+        ],
+        compiler_params=pltpu.CompilerParams(
+            collective_id=0, has_side_effects=True, vmem_limit_bytes=48 * 2**20
+        ),
+        name="decode_attention",
+    )(
+        activations,
+        norm_gain[None],
+        block_list.reshape(rows, -1),
+        block_slot_table,
+        kept_len,
+        w_query,
+        w_out,
+        key_pool,
+        value_block_store,
+    )
+
+
+def per_device(*arrays):
+    activations, _, w_query, w_out, key_pool = arrays[:5]
+    lenders, tensors = lax.axis_size("lender"), lax.axis_size("tensor")
+    rows = activations.shape[0]
+    kv_heads, slot_count, tokens, head_dim = key_pool.shape
+    columns, out_width = w_query.shape[1], w_out.shape[1]
+    width = columns // lenders
+    fits = (
+        rows == SUBLANES
+        and head_dim == LANES
+        and tokens == LANES
+        and columns % (lenders * head_dim) == 0
+        and columns // kv_heads % max(width, 1) == 0
+        and width * rows % (2 * SUBLANES * head_dim) == 0
+        and width * rows <= LANES * head_dim
+        and rows % tensors == 0
+        and out_width % (tensors * LANES) == 0
+        and slot_count * tokens % 512 == 0
+    )
+    return (fused if fits else separate_ops)(*arrays)
+
+
 def solution(mesh):
     in_specs = (
         P("group", "lender"),

time: 116 us -> 35.6 us (0.31)
  blocking collectives: 37.3 us -> 0 us
  waiting for transfers between devices: 31 us -> 0 us
  Pallas kernels: 0 us -> 27.8 us
  between operations: 14.2 us -> 0.01 us
  matrix products: 14 us -> 0 us
  starting transfers between devices: 9.95 us -> 0 us
  other arithmetic: 2.96 us -> 0 us
    pallas_call x0 -> x1, Pallas kernels: none -> 27.8 us  [fused(): pl.pallas_call(functools.partial(fused_kernel, lenders, tensors), out_sha...]
    psum x1 -> x0, waiting for transfers between devices: 18.7 us -> none  [per_device(): projected, square_sum = lax.psum((partial_value, squares), 'lender')]
    dot_general x7 -> x0, matrix products: 14 us -> none  [the longest x1 5.24 us: per_device(): partial_value = jnp.dot(scaled, w_query, preferred_element_type=jnp.float32)]
    psum x1 -> x0, blocking collectives: 13.5 us -> none  [per_device(): projected, square_sum = lax.psum((partial_value, squares), 'lender')]
    all_gather x1 -> x0, blocking collectives: 13.1 us -> none  [per_device(): attended = lax.all_gather(home_attended, 'lender', axis=0, tiled=True)]
    all_to_all x3 -> x0, waiting for transfers between devices: 12.3 us -> none  [the longest x1 5.51 us: per_device(): lax.all_to_all(row_value, 'lender', split_axis=0, concat_axis=0, tiled=True)]
    unnamed x1 -> x0, blocking collectives: 10.7 us -> none
    all_to_all x3 -> x0, starting transfers between devices: 9.92 us -> none  [the longest x1 3.39 us: per_device(): lax.all_to_all(row_high, 'lender', split_axis=0, concat_axis=0, tiled=True)]
  transfers between devices with their start and end apart: 4 -> 0, of which waited for: 4 -> 0; matrix products, arithmetic and copies ran while one was open for 7% -> 0% of each run, Pallas kernels for 0% -> 0%
where the time goes in v1:
time: 35.6 us; the launch traced here: 35.2 us
  Pallas kernels  27.8 us (78%)
  local copies, waits for them, and re-layouts  7.44 us (21%)
    pallas_call x1, Pallas kernels, fused(): pl.pallas_call(functools.partial(fused_kernel, lenders, tensors), out_sha...  27.8 us
    unnamed x10, local copies, waits for them, and re-layouts  5.97 us
    reshape x1, local copies, waits for them, and re-layouts, fused(): block_list.reshape(rows, -1)  0.77 us

profile of v1, /device:TPU:0, one launch (start us, length us, event | category | flops | bytes accessed | tf_op | source)
XLA Modules:
  0.0 35.2 jit_solution(14332357171036309444)
XLA Ops:
  0.0 0.8 %reshape.3.list_ref = s32[8,32]{1,0:T(8,128)S(1)} reshape(s32[8,2,16]{2,1,0:T(2,128)} %param.15) | data formatting | bytes 2048 | tf_op jit(solution)/shard_map/reshape | solution.py:457
  0.8 0.8 %copy.10.kept_ref = s32[8,2]{1,0:T(8,128)S(1)} copy(s32[8,2]{0,1:T(2,128)} %param.17) | data formatting | bytes 128 | tf_op args[8]
  1.5 0.7 %broadcast_in_dim.3.gain_ref = bf16[1,2048]{1,0:T(2,128)(2,1)S(1)} reshape(bf16[2048]{0:T(1024)(128)(2,1)} %param.10) | data formatting | bytes 8192 | tf_op jit(solution)/shard_map/broadcast_in_dim | solution.py:456
  2.2 0.0 copy-start
  2.2 1.6 %copy-done = bf16[2,32,128,128]{3,2,1,0:T(8,128)(2,1)S(1)} copy-done((bf16[2,32,128,128]{3,2,1,0:T(8,128)(2,1)S(1)}, bf16[2,32,128,128]{3,2,1,0:T(8,128)(2,1)}, u32[]{:S(2)}) %copy-start) | copy-done | bytes 2097176
  3.8 0.0 copy-start.1
  3.8 1.6 %copy-done.1 = bf16[2,32,128,128]{3,2,1,0:T(8,128)(2,1)S(1)} copy-done((bf16[2,32,128,128]{3,2,1,0:T(8,128)(2,1)S(1)}, bf16[2,32,128,128]{3,2,1,0:T(8,128)(2,1)}, u32[]{:S(2)}) %copy-start.1) | copy-done | bytes 2097176
  5.4 0.0 copy-start.2
  5.4 0.8 %copy-done.2 = bf16[8,2048]{1,0:T(8,128)(2,1)S(1)} copy-done((bf16[8,2048]{1,0:T(8,128)(2,1)S(1)}, bf16[8,2048]{1,0:T(8,128)(2,1)}, u32[]{:S(2)}) %copy-start.2) | copy-done | bytes 32792
  6.2 0.0 copy-start.3
  6.2 0.7 %copy-done.3 = s32[2,128]{1,0:T(2,128)S(1)} copy-done((s32[2,128]{1,0:T(2,128)S(1)}, s32[2,128]{1,0:T(2,128)}, u32[]{:S(2)}) %copy-start.3) | copy-done | bytes 1048
  6.8 27.8 %decode_attention.1 = bf16[2,2048]{1,0:T(2,128)(2,1)S(1)} custom-call(bf16[8,2048]{1,0:T(8,128)(2,1)S(1)} %copy-done.2, bf16[1,2048]{1,0:T(2,128)(2,1)S(1)} %broadcast_in_dim.3.gain_ref, s32[8,32]{1,0:T(8,128)S(1)} %reshape.3.list_ref, s32[2,128]{1,0:T(2,128)S(1)} %copy-done.3, s32[8,2]{1,0:T(8,128)S(1)} %copy.10.kept_ref, bf16[2048,2048]{1,0:T(8,128)(2,1)} %wq_hbm.1, ...), custom_call_target="tpu_custom_call" | custom-call | tf_op jit(solution)/shard_map/decode_attention/pallas_call | solution.py:422
  34.6 0.6 %copy.12 = bf16[2,2048]{1,0:T(2,128)(2,1)} copy(bf16[2,2048]{1,0:T(2,128)(2,1)S(1)} %decode_attention.1) | data formatting | bytes 16384
Async XLA Ops:
  2.2 1.6 %copy-start = (bf16[2,32,128,128]{3,2,1,0:T(8,128)(2,1)S(1)}, bf16[2,32,128,128]{3,2,1,0:T(8,128)(2,1)}, u32[]{:S(2)}) copy-start(bf16[2,32,128,128]{3,2,1,0:T(8,128)(2,1)} %key_hbm.1) | copy-start | bytes 6291460
  3.8 1.6 %copy-start.1 = (bf16[2,32,128,128]{3,2,1,0:T(8,128)(2,1)S(1)}, bf16[2,32,128,128]{3,2,1,0:T(8,128)(2,1)}, u32[]{:S(2)}) copy-start(bf16[2,32,128,128]{3,2,1,0:T(8,128)(2,1)} %value_hbm.1) | copy-start | bytes 6291460
  5.4 0.8 %copy-start.2 = (bf16[8,2048]{1,0:T(8,128)(2,1)S(1)}, bf16[8,2048]{1,0:T(8,128)(2,1)}, u32[]{:S(2)}) copy-start(bf16[8,2048]{1,0:T(8,128)(2,1)} %act_ref.1) | copy-start | bytes 98308
  6.2 0.7 %copy-start.3 = (s32[2,128]{1,0:T(2,128)S(1)}, s32[2,128]{1,0:T(2,128)}, u32[]{:S(2)}) copy-start(s32[2,128]{1,0:T(2,128)} %table_ref.1) | copy-start | bytes 3076
